TPU v7x, 32 devices: a whole 2x2x4 slice. The times are simulated.
32 devices in a mesh: prow: 8 (over y, x, core), pcol: 4 (over z).
Axes of the slice: x: 2, y: 2, z: 4, core: 2. Of those that a mesh axis runs over, the one named last changes fastest.
Arguments:
- rhs_panel: float32 [2048, 2, 256], P(('prow', 'pcol')), may hold values from -6 to 6
- pivots: int32 [2048], replicated, may hold values from 0 to 2047, each once
- diag_inverse: float32 [2048, 2, 2048], P('pcol'), may hold values from -1 to 2, as said below
- panel_column: float32 [2048, 2, 2048], P('prow', None, 'pcol'), may hold values from -0.09375 to 0.09375
- trailing: float32 [2048, 2, 256], P(('prow', 'pcol')), may hold values from -6 to 6
- derivative: float32 [2048, 2, 256], P('pcol'), may hold values from -4 to 4
Outputs:
- updated: float32 [2048, 2, 256], P(('prow', 'pcol'))
- adjoint_panel: float32 [2048, 2, 256], P('pcol')
- sensitivity: float32 [256], replicated
Inputs may be any that keep to these rules, and one draw needn't show every extreme that they name: `diag_inverse`: zero above the diagonal in both parts; diagonal real parts between 0.5 and 1.5. `pivots`: each of 0 to 2047 once.
All inputs are finite; a program needn't handle non-finite values.
Results may differ from a plain program's by a relative error of at most 0.00017.
Values sent between devices are 32-bit elements; how exact they have to be, the bound alone decides.
No kernel may reach another device: no remote copies, remote signals or barrier semaphores. Data moves between devices by JAX's collectives and lax.ppermute only.
A program may use at most 64 MiB of HBM per device.

v0:
```python
import jax
import jax.numpy as jnp
from jax import lax
from jax.sharding import PartitionSpec as P


def complex_product(lhs, rhs):
    count_rows = lhs.shape[0]
    inner = lhs.shape[2]
    flat = lhs.reshape(count_rows, 2 * inner)
    real_part = rhs[:, 0, :]
    imag_part = rhs[:, 1, :]
    stacked = jnp.concatenate(
        [
            jnp.concatenate([real_part, imag_part], axis=1),
            jnp.concatenate([-imag_part, real_part], axis=1),
        ],
        axis=0,
    )
    result = jnp.dot(
        flat, stacked, preferred_element_type=jnp.float32, precision=lax.Precision.HIGHEST
    )
    return result.reshape(count_rows, 2, rhs.shape[2])


def per_device(rhs_panel, pivots, diag_inverse, panel_column, trailing, derivative):
    inverse_order = jnp.argsort(pivots)
    permuted = jnp.take(diag_inverse, inverse_order, axis=2)
    block = permuted
    solved = complex_product(block, lax.all_gather(rhs_panel, ("prow", "pcol"), axis=0, tiled=True))
    block = panel_column
    correction = lax.psum_scatter(
        complex_product(block, solved), "pcol", scatter_dimension=0, tiled=True
    )
    updated = trailing - correction
    local_terms = -jnp.sum(solved * derivative, axis=(0, 1))
    sensitivity = lax.psum(local_terms, "pcol")
    return (updated, solved, sensitivity)


def solution(mesh):
    in_specs = (
        P(("prow", "pcol"), None, None),
        P(),
        P("pcol", None, None),
        P("prow", None, "pcol"),
        P(("prow", "pcol"), None, None),
        P("pcol", None, None),
    )
    out_specs = (P(("prow", "pcol"), None, None), P("pcol", None, None), P())
    return jax.shard_map(
        per_device, mesh=mesh, in_specs=in_specs, out_specs=out_specs, check_vma=False
    )
```

profile of v0, /device:TPU:0, one launch (start us, length us, event | category | flops | bytes accessed | tf_op | source)
XLA Modules:
  0.0 165.2 jit_solution(6676639049891514944)
XLA Ops:
  7.2 0.0 all-gather.2.cloned.1.call-start
  7.2 1.6 copy.30
  8.8 0.0 all-gather.2.cloned.1.call-update
  8.8 0.0 copy-start.5
  8.8 0.0 all-reduce.3.cloned.1.call-start
  8.9 17.1 %copy.28 = f32[512,2,2048]{0,1,2:T(2,128)} copy(f32[512,2,2048]{2,1,0:T(2,128)} %param.8) | data formatting | bytes 16777216 | tf_op args[2]
  26.0 0.0 copy-done.5
  26.0 5.0 %sort.17 = (s32[2048]{0:T(1024)}, s32[2048]{0:T(1024)S(1)}) sort(s32[2048]{0:T(1024)S(1)} %copy-done.5, s32[2048]{0:T(1024)S(1)} %iota.4), dimensions={0}, to_apply=%region_0.0 | sort | flops 22528 | bytes 32768 | tf_op jit(solution)/shard_map/jit(argsort)/sort | solution.py:27
  31.0 26.3 %gather_fusion = f32[2048,512,2]{1,2,0:T(2,128)} fusion(f32[512,2,2048]{0,1,2:T(2,128)} %copy.28, s32[2048]{0:T(1024)S(1)} %fusion.8), kind=kCustom, calls=%fused_computation | custom fusion | bytes 16785408 | tf_op jit(solution)/shard_map/jit(_take)/gather | solution.py:28
  57.3 9.0 %select_bitcast_fusion = f32[512,2,2048]{0,1,2:T(2,128)S(1)} fusion(f32[2048,512,2]{1,2,0:T(2,128)} %gather_fusion, pred[2048]{0:T(1024)(128)(4,1)S(1)} %compare_and_fusion), kind=kLoop, calls=%fused_computation.2 | loop fusion | flops 2097152 | bytes 16779264 | tf_op jit(solution)/shard_map/jit(_take)/select_n | solution.py:28
  66.3 0.0 copy-start.1
  66.3 0.0 copy-start.2
  66.4 4.7 %copy.29 = f32[512,2,2048]{0,2,1:T(8,128)} copy(f32[512,2,2048]{0,1,2:T(2,128)S(1)} %select_bitcast_fusion) | data formatting | bytes 16777216 | tf_op jit(solution)/shard_map/jit(_take)/select_n | solution.py:28
  71.1 0.8 copy.34
  71.9 1.2 copy.38
  73.1 3.4 %all-gather.2.cloned.1.call-done = f32[2048,2,256]{2,0,1:T(8,128)} async-done(((f32[64,2,256]{2,0,1:T(8,128)}), f32[2048,2,256]{2,0,1:T(8,128)}) %all-gather.2.cloned.1.call-update) | async-done | bytes 4194320 | tf_op jit(solution)/shard_map/all_gather | solution.py:30
  76.5 4.6 %slice_bitcast_fusion = (f32[2048,256]{1,0:T(8,128)}, f32[2048,256]{1,0:T(8,128)}) fusion(f32[2048,2,256]{2,0,1:T(8,128)} %all-gather.2.cloned.1.call-done), kind=kLoop, calls=%fused_computation.3 | loop fusion | bytes 8388608 | tf_op jit(solution)/shard_map/squeeze | solution.py:12
  81.1 1.5 fusion.11
  82.6 7.8 %maximum_bitcast_fusion = f32[512,4096]{0,1:T(8,128)} fusion(f32[2048,256]{1,0:T(8,128)} %get-tuple-element.18, f32[2048,256]{1,0:T(8,128)} %fusion.11, f32[2048,256]{1,0:T(8,128)} %get-tuple-element.17), kind=kLoop, calls=%fused_computation.1 | loop fusion | flops 6291456 | bytes 14680064 | tf_op jit(solution)/shard_map/dot_general | solution.py:20
  90.4 8.9 %copy.31 = f32[512,4096]{1,0:T(8,128)} copy(f32[512,4096]{0,1:T(8,128)} %maximum_bitcast_fusion) | data formatting | bytes 16777216 | tf_op jit(solution)/shard_map/dot_general | solution.py:20
  99.3 16.8 %multiply_reduce_fusion = (f32[256]{0:T(256)S(1)}, f32[512,2,256]{0,2,1:T(8,128)S(1)}) fusion(f32[512,2,256]{0,2,1:T(8,128)S(1)} %copy.34, f32[512,4096,1]{0,1,2:T(8,128)} %bitcast.29, f32[2,256,4096]{2,1,0:T(8,128)} %bitcast.30), kind=kOutput, calls=%fused_computation.13 | convolution fusion | flops 12885426176 | bytes 18875392 | tf_op jit(solution)/shard_map/dot_general | solution.py:20
  116.1 0.0 copy-start.6
  116.1 0.0 copy-start.4
  116.1 0.1 slice_bitcast_fusion.2
  116.3 1.9 %fusion = f32[512,256]{1,0:T(8,128)S(1)} fusion(f32[256,1024]{1,0:T(8,128)S(1)} %bitcast.32, f32[512,256]{0,1:T(8,128)S(1)} %get-tuple-element.20, f32[512,256]{0,1:T(8,128)S(1)} %fusion.10, f32[512,256]{0,1:T(8,128)S(1)} %get-tuple-element.19), kind=kOutput, calls=%fused_computation.5 | convolution fusion | flops 1612185600 | bytes 3145728 | tf_op jit(solution)/shard_map/dot_general | solution.py:20
  118.1 1.0 copy.33
  119.2 0.0 all-reduce.3.cloned.1.call-update
  119.2 0.6 dynamic-slice
  120.4 1.3 copy.35
  121.7 11.1 %psum.7 = f32[256]{0:T(256)} all-reduce(f32[256]{0:T(256)S(1)} %neg.11), channel_id=1, replica_groups=mesh['prow'=8,'pcol'=4] {'pcol'}, use_global_device_ids=true, to_apply=%region_3.4 | all-reduce | flops 256 | bytes 2048 | tf_op jit(solution)/shard_map/psum | solution.py:37
  132.8 23.9 %all-reduce.3.cloned.1.call-done = f32[256,2,256]{2,1,0:T(2,128)} async-done(((f32[256,2,256]{2,1,0:T(2,128)}), f32[256,2,256]{2,1,0:T(2,128)}) %all-reduce.3.cloned.1.call-update) | async-done | bytes 524304
  156.8 1.6 dynamic-slice_subtract_fusion
  (13 shorter events, 0.1 us)
Async XLA Ops:
  7.2 69.3 %all-gather.2.cloned.1.call-start = ((), (), s32[]{:S(2)}) async-start(), calls=%async_computation | async-start | bytes 4325376 | tf_op jit(solution)/shard_map/all_gather | solution.py:30
  8.8 17.2 %copy-start.5 = (s32[2048]{0:T(1024)S(1)}, s32[2048]{0:T(1024)}, u32[]{:S(2)}) copy-start(s32[2048]{0:T(1024)} %param.7) | copy-start | bytes 24580
  8.8 147.9 %all-reduce.3.cloned.1.call-start = ((), (), s32[]{:S(2)}) async-start(), calls=%async_computation.1 | async-start | bytes 1048576
  66.3 4.8 %copy-start.1 = (f32[512,2,256]{2,1,0:T(2,128)S(1)}, f32[512,2,256]{2,1,0:T(2,128)}, u32[]{:S(2)}) copy-start(f32[512,2,256]{2,1,0:T(2,128)} %param.11) | copy-start | bytes 3145732
  66.3 5.6 %copy-start.2 = (f32[256,2,512]{2,1,0:T(2,128)S(1)}, f32[256,2,512]{2,1,0:T(2,128)}, u32[]{:S(2)}) copy-start(f32[256,2,512]{2,1,0:T(2,128)} %param.9) | copy-start | bytes 3145732
  76.5 4.6 %copy-start = (f32[2048,2,256]{2,0,1:T(8,128)S(1)}, f32[2048,2,256]{2,0,1:T(8,128)}, u32[]{:S(2)}) copy-start(f32[2048,2,256]{2,0,1:T(8,128)} %all-gather.2.cloned.1.call-done) | copy-start | bytes 12582916
  99.3 16.9 %copy-start.3 = (f32[32,8,2,512]{3,1,2,0:T(8,128)S(1)}, f32[32,8,2,512]{3,1,2,0:T(8,128)}, u32[]{:S(2)}) copy-start(f32[32,8,2,512]{3,1,2,0:T(8,128)} %copy.38) | copy-start | bytes 3145732
  116.1 3.1 %copy-start.6 = (u32[32]{0:T(128)S(1)}, u32[32]{0:T(128)}, u32[]{:S(2)}) copy-start(u32[32]{0:T(128)} %constant.20) | copy-start | bytes 388
  116.1 40.6 %copy-start.4 = (f32[64,2,256]{2,1,0:T(2,128)S(1)}, f32[64,2,256]{2,1,0:T(2,128)}, u32[]{:S(2)}) copy-start(f32[64,2,256]{2,1,0:T(2,128)} %param.10) | copy-start | bytes 393220
Sparse Core Ops, SparseCore 0:
  11.6 64.8 all-gather.1
  119.3 37.4 all-reduce.2
where the time goes:
time: 166 us; the launch traced here: 165 us
  local copies, waits for them, and re-layouts  68.2 us (41%)
  waiting for transfers between devices  27.4 us (17%)
  other arithmetic  25.1 us (15%)
  matrix products  18.6 us (11%)
  between operations  14.8 us (9%)
  blocking collectives  11.1 us (7%)
    gather x1, local copies, waits for them, and re-layouts, per_device(): permuted = jnp.take(diag_inverse, inverse_order, axis=2)  26.3 us
    unnamed x3, waiting for transfers between devices  24 us
    unnamed x20, local copies, waits for them, and re-layouts  22.6 us
    dot_general x2, matrix products, complex_product(): jnp.dot(flat, stacked, preferred_element_type=jnp.float32, precision=lax....  18.6 us
    psum x1, blocking collectives, per_device(): sensitivity = lax.psum(local_terms, 'pcol')  11.1 us
    select_n x1, other arithmetic, per_device(): permuted = jnp.take(diag_inverse, inverse_order, axis=2)  9.03 us
    dot_general x1, local copies, waits for them, and re-layouts, complex_product(): jnp.dot(flat, stacked, preferred_element_type=jnp.float32, precision=lax....  8.92 us
    dot_general x1, other arithmetic, complex_product(): jnp.dot(flat, stacked, preferred_element_type=jnp.float32, precision=lax....  7.84 us
  transfers between devices with their start and end apart: 2, of which 2 were waited for; matrix products, arithmetic and copies ran while one was open for 40% of the time, Pallas kernels for 0%

commit v1 on v0

v1 whole, which is shorter than its diff:
```python
import functools

import jax
import jax.numpy as jnp
from jax import lax
from jax.experimental import pallas as pl
from jax.experimental.pallas import tpu as pltpu
from jax.sharding import Mesh
from jax.sharding import PartitionSpec as P

F32 = jnp.float32
BF16 = jnp.bfloat16
LANES = 128
MIB = 1 << 20

SMEM = pl.BlockSpec(memory_space=pltpu.SMEM)
VMEM = pl.BlockSpec(memory_space=pltpu.VMEM)
ANY = pl.BlockSpec(memory_space=pl.ANY)
HBM = pl.BlockSpec(memory_space=pltpu.HBM)
PITCH = 40
LONG = (1 << 33, 1 << 20)
OTHERS = (3, 1, 2)
SHIFTS = (0, 1, 3, 2)
sds = jax.ShapeDtypeStruct


def to_rows(x):
    a, b, c = x.shape
    tiles = c // LANES
    return x.reshape(a, b, tiles, LANES).transpose(0, 2, 1, 3).reshape(a * tiles * b, LANES)


def from_rows(x, a, b, c):
    tiles = c // LANES
    return x.reshape(a, tiles, b, LANES).transpose(0, 2, 1, 3).reshape(a, b, c)


def left_half(shape):
    return lax.broadcasted_iota(jnp.int32, shape, 1) < 64


def other_half(x):
    return pltpu.roll(x, 64, 1)


def split(x):
    high = x.astype(BF16)
    low = (x - high.astype(F32)).astype(BF16)
    return high, low


def here(axis):
    return lax.axis_index(axis)


def pack_kernel(rhs_ref, o0, o1, o2, o3, blocks_ref):
    for j in range(2):
        re = rhs_ref[pl.ds(2 * j, 64, stride=4), :]
        im = rhs_ref[pl.ds(2 * j + 1, 64, stride=4), :]
        first = left_half(re.shape)
        blocks_ref[2 * j] = jnp.where(first, re, other_half(im))
        blocks_ref[2 * j + 1] = jnp.where(first, other_half(re), im)
    for d, out in enumerate((o0, o1, o2, o3)):
        out[...] = blocks_ref[lax.bitwise_xor(here("chip"), d)]


def chunk_kernel(after_ref, b0, b3, b1, b2, out_ref):
    del after_ref
    for d, block in enumerate((b0, b1, b2, b3)):
        at = pl.multiple_of(lax.bitwise_xor(here("chip"), d) * 64, 64)
        out_ref[pl.ds(at, 64), :] = block[...]


def diag_copies(first, d_ref, held_ref, sems):
    copies = []
    for i in range(2):
        source = pl.multiple_of(here("core") * 256 + first + i * 64, 64)
        target = held_ref.at[pl.ds(i * 64, 64), pl.ds(0, 32)]
        copies.append(pltpu.make_async_copy(d_ref.at[pl.ds(source, 64)], target, sems.at[i]))
        copies[i].start()
    return copies


def diag_split(copies, held_ref, parts_ref):
    flat_ref = held_ref.reshape(128 * PITCH, LANES)
    for i, copy in enumerate(copies):
        copy.wait()
        for j in range(16):
            for c in range(2):
                x = flat_ref[pl.ds(i * 64 * PITCH + 2 * j + c, 64, stride=PITCH), :]
                for e, part in enumerate(split(x)):
                    row = c * 256 + e * 128 + i * 64
                    parts_ref[row : row + 64, j * LANES : (j + 1) * LANES] = part


def diag_kernel(d_ref, parts_ref, held_ref, sems):
    diag_split(diag_copies(0, d_ref, held_ref, sems), held_ref, parts_ref)


def diag_inverse_kernel(pivots_hbm, d_ref, m0, parts_ref, inverse_ref, part_ref, held_ref, sems, pivots_ref, sem):
    pivots_copy = pltpu.make_async_copy(pivots_hbm, pivots_ref, sem)
    pivots_copy.start()
    copies = diag_copies(128, d_ref, held_ref, sems)
    pivots_copy.wait()

    def invert(step, _):
        for e in range(16):
            i = step * 16 + e
            inverse_ref[pivots_ref[i]] = i
        return 0

    lax.fori_loop(0, 128, invert, 0)
    scatter_rows(inverse_ref, m0, here("core"), SHIFTS[0], part_ref)
    diag_split(copies, held_ref, parts_ref)


def panel_kernel(x_ref, derivative_ref, high_ref, low_ref, packed_ref):
    for j in range(4):
        for c in range(2):
            high, low = split(x_ref[pl.ds(2 * j + c, 256, stride=8), :])
            high_ref[c, :, j * LANES : (j + 1) * LANES] = high
            low_ref[c, :, j * LANES : (j + 1) * LANES] = low
    for j in range(2):
        re = derivative_ref[pl.ds(2 * j, 512, stride=4), :]
        im = derivative_ref[pl.ds(2 * j + 1, 512, stride=4), :]
        first = left_half(re.shape)
        packed_ref[2 * j] = jnp.where(first, re, other_half(im))
        packed_ref[2 * j + 1] = jnp.where(first, other_half(re), im)


def scatter_rows(inverse_ref, chunk, core, t, ordered_ref):
    z = lax.rem(here("pcol") - t + 4, 4)

    def body(step, _):
        first = lax.div(step, 4) * 512 + lax.rem(step, 4) * 16 + core * 256 + z * 64
        for e in range(16):
            ordered_ref[inverse_ref[first + e]] = chunk[step * 16 + e]
        return 0

    lax.fori_loop(0, 16, body, 0)


def fetch(*copies):
    copies = [pltpu.make_async_copy(*copy) for copy in copies]
    for copy in copies:
        copy.start()
    for copy in copies:
        copy.wait()


def relay_kernel(after_ref, x_ref, out_ref):
    del after_ref
    out_ref[...] = x_ref[...]


def bundle_kernel(after_ref, a_ref, b_ref, out_ref):
    del after_ref
    out_ref[0:256, :] = a_ref[...]
    out_ref[256:512, :] = b_ref[...]


def scatter_kernel(names, inverse_hbm, part_hbm, *rest):
    *operands, out_ref, inverse_ref, sem, part_sem = rest
    fetch((inverse_hbm, inverse_ref, sem), (part_hbm, out_ref, part_sem))
    for chunks, operand in zip(names, operands):
        for i, (c, t) in enumerate(chunks):
            chunk = operand.at[i * 256 : (i + 1) * 256]
            scatter_rows(inverse_ref, chunk, lax.bitwise_xor(here("core"), c), t, out_ref)


def solve_kernel(ordered_ref, first_ref, second_ref, out_ref):
    weights = jnp.concatenate(split(ordered_ref[...]), axis=1)
    for i, parts_ref in enumerate((first_ref, second_ref)):
        f = jnp.dot(parts_ref[...], weights, preferred_element_type=F32)
        f = f[:, :LANES] + f[:, LANES:]
        re, im = f[0:128] + f[128:256], f[256:384] + f[384:512]
        cross = other_half(im)
        out_ref[i * 128 : (i + 1) * 128, :] = re + jnp.where(left_half(cross.shape), -cross, cross)


def half_product(members, h, xs, panel_refs, split_refs):
    ph_ref, pl_ref, derivative_ref = panel_refs
    sh_ref, sl_ref = split_refs
    at = pl.multiple_of(lax.bitwise_xor(here("core"), h) * 256, 256)
    row = lax.broadcasted_iota(jnp.int32, (8, LANES), 0)
    tail = jnp.zeros((8, LANES), F32)
    for i, (d, x) in enumerate(zip(members, xs)):
        chip = lax.bitwise_xor(here("chip"), d)
        total = jnp.sum((x * derivative_ref[chip, pl.ds(at, 256), :]).reshape(32, 8, LANES), axis=0)
        tail = jnp.where(row == i, jnp.sum(total, axis=0, keepdims=True), tail)
        columns = slice(i * LANES, (i + 1) * LANES)
        sh_ref[:, columns], sl_ref[:, columns] = split(x)
    f = []
    for c in range(2):
        high, low = ph_ref[c, :, pl.ds(at, 256)], pl_ref[c, :, pl.ds(at, 256)]
        x = jnp.dot(high, sh_ref[...], preferred_element_type=F32)
        x += jnp.dot(high, sl_ref[...], preferred_element_type=F32)
        f.append(x + jnp.dot(low, sh_ref[...], preferred_element_type=F32))
    return f, tail


def half_kernel(members, ph_ref, pl_ref, derivative_ref, *rest):
    *blocks, f_ref, tail_ref, sh_ref, sl_ref = rest
    xs = [block[...] for block in blocks]
    f, tail_ref[...] = half_product(members, 0, xs, (ph_ref, pl_ref, derivative_ref), (sh_ref, sl_ref))
    f_ref[0], f_ref[1] = f


def rest_kernel(members, ph_ref, pl_ref, derivative_ref, f_ref, tail_ref, theirs_ref, *rest):
    *outs, sh_ref, sl_ref, corr_ref = rest[-7:]
    count = len(members)
    xs = [theirs_ref[i * 256 : (i + 1) * 256, :] for i in range(count)]
    f, tail = half_product(members, 1, xs, (ph_ref, pl_ref, derivative_ref), (sh_ref, sl_ref))
    f = [f[0] + f_ref[0], f[1] + f_ref[1]]
    tail += tail_ref[...]
    for out in outs:
        out[count * 64 : count * 64 + 8, :] = tail
    for i in range(count):
        columns = slice(i * LANES, (i + 1) * LANES)
        cross = other_half(f[1][:, columns])
        corr_ref[i] = f[0][:, columns] + jnp.where(left_half(cross.shape), -cross, cross)
        for t, out in enumerate(outs):
            base = pl.multiple_of(lax.rem(here("pcol") + t, 4) * 64, 64)
            out[i * 64 : (i + 1) * 64, :] = corr_ref[i, pl.ds(base, 64), :]


def forward_kernel(after_ref, b0, b1, b2, out_ref):
    del after_ref
    for i, block in enumerate((b0, b1, b2)):
        out_ref[i * 256 : (i + 1) * 256, :] = block[...]


def store_tiles(held_ref, out_ref, first_row, count):
    for j in range(2):
        a, b = held_ref[2 * j], held_ref[2 * j + 1]
        first = left_half(a.shape)
        out_ref[pl.ds(first_row + 2 * j, count, stride=4), :] = jnp.where(first, a, other_half(b))
        out_ref[pl.ds(first_row + 2 * j + 1, count, stride=4), :] = jnp.where(first, other_half(a), b)


def adjoint_kernel(m0, m1, m2, m3, own_ref, others_ref, adjoint_ref, held_ref):
    core = here("core")
    for c in range(2):
        for d, block in enumerate((m0, m1, m2, m3)):
            if c == 1:
                i = OTHERS.index(d) if d else 0
                block = others_ref.at[i * 256 : (i + 1) * 256, :] if d else own_ref
            held_ref[lax.bitwise_xor(here("chip"), d)] = block[...]
        store_tiles(held_ref, adjoint_ref, pl.multiple_of(lax.bitwise_xor(core, c) * 1024, 1024), 256)


def sum_kernel(count, i0, i1, i2, i3, rows_ref, sums_ref, tails_ref):
    pieces = (i0, i1, i2, i3)
    rows = slice(0, count * 64)
    rows_ref[...] = (i0[rows, :] + i1[rows, :]) + (i2[rows, :] + i3[rows, :])
    for t, piece in enumerate(pieces):
        tails_ref[lax.rem(here("pcol") - t + 4, 4)] = piece[count * 64 : count * 64 + 8, :]
    value = -((tails_ref[0] + tails_ref[1]) + (tails_ref[2] + tails_ref[3]))
    sums_ref[...] = value + other_half(value)


def final_kernel(
    trailing_ref, own_rows, own_sums, b0, b1, b2, b3, updated_ref, sensitivity_ref,
    rows_ref, group_ref, tails_ref, held_ref, sums_ref,
):
    sum_kernel(3, b0, b1, b2, b3, rows_ref, group_ref, tails_ref)
    for d in range(4):
        chip = lax.bitwise_xor(here("chip"), d)
        i = OTHERS.index(d) if d else 0
        rows = rows_ref[i * 64 : (i + 1) * 64, :] if d else own_rows[...]
        sums = group_ref[i : i + 1, :] if d else own_sums[0:1, :]
        held_ref[chip] = rows
        sums_ref[chip] = sums
    for j in range(2):
        a, b = held_ref[2 * j], held_ref[2 * j + 1]
        first = left_half(a.shape)
        at = pl.ds(2 * j, 64, stride=4)
        updated_ref[at, :] = trailing_ref[at, :] - jnp.where(first, a, other_half(b))
        at = pl.ds(2 * j + 1, 64, stride=4)
        updated_ref[at, :] = trailing_ref[at, :] - jnp.where(first, other_half(a), b)
        sensitivity_ref[j : j + 1, :] = jnp.where(left_half((1, LANES)), sums_ref[2 * j], sums_ref[2 * j + 1])


def crossed(x, axis, count, d):
    return lax.ppermute(x, axis, [(i, i ^ d) for i in range(count)])


def shifted(x, axis, count, t):
    return lax.ppermute(x, axis, [(i, (i + t) % count) for i in range(count)])


def call(kernel, operands, in_specs, outs, scratch=(), mib=4, cost=None):
    return pl.pallas_call(
        kernel,
        in_specs=in_specs,
        out_specs=[SMEM if o.dtype == jnp.int32 else VMEM for o in outs],
        out_shape=outs,
        scratch_shapes=list(scratch),
        compiler_params=pltpu.CompilerParams(vmem_limit_bytes=mib * MIB),
        cost_estimate=cost and pl.CostEstimate(flops=cost[0], bytes_accessed=cost[1], transcendentals=0),
    )(*operands)


def per_device(rhs_panel, pivots, diag_inverse, panel_column, trailing, derivative):
    def rows(count):
        return sds((count, LANES), F32)

    def buffer(*shape, dtype=F32):
        return pltpu.VMEM(shape, dtype)

    inverse_scratch = [pltpu.SMEM((2048,), jnp.int32), pltpu.SemaphoreType.DMA]

    panel = sds((2, 256, 512), BF16)
    ph, pl_, derivative_packed = call(
        panel_kernel, [to_rows(panel_column), to_rows(derivative)], [VMEM] * 2,
        [panel, panel, sds((4, 512, LANES), F32)], cost=(1 << 21, 4 << 20),
    )

    half = sds((512, 2048), BF16)
    diagonal_rows = to_rows(diag_inverse).reshape(512, 32, LANES)
    held = [buffer(128, PITCH, LANES), pltpu.SemaphoreType.DMA((2,))]
    (first_half,) = call(diag_kernel, [diagonal_rows], [HBM], [half], held, mib=48, cost=(1 << 22, 4 << 20))

    packed = call(pack_kernel, [to_rows(rhs_panel)], [VMEM], [rows(64)] * 4, [buffer(4, 64, LANES)], cost=LONG)
    arrived = [crossed(packed[d], "chip", 4, d) for d in (3, 1, 2)]
    (chunk,) = call(chunk_kernel, [first_half, packed[0], *arrived], [ANY] + [VMEM] * 4, [rows(256)], cost=LONG)
    mine = [chunk] + [shifted(chunk, "pcol", 4, t) for t in SHIFTS[1:]]

    def single(x):
        return x.reshape(x.shape[0], 1, LANES)

    def relay(after, x, cost):
        return call(relay_kernel, [after, x], [ANY, VMEM], [rows(x.shape[0])], cost=cost)[0]

    def scatter(part, *named):
        return call(
            functools.partial(scatter_kernel, [n for n, _ in named]),
            [inverse, part, *[single(x) for _, x in named]], [ANY] * 2 + [VMEM] * len(named),
            [ordered], [*inverse_scratch, pltpu.SemaphoreType.DMA], cost=(1 << 20, 1 << 20),
        )[0]

    ordered = sds((2048, 1, LANES), F32)
    second_half, inverse, part = call(
        diag_inverse_kernel, [pivots, diagonal_rows, single(chunk)], [ANY, HBM, VMEM],
        [half, sds((2048,), jnp.int32), ordered], held + inverse_scratch, mib=46, cost=(1 << 22, 4 << 20),
    )
    a, b, c = SHIFTS[1:]
    (bundle,) = call(bundle_kernel, [second_half, chunk, mine[1]], [ANY, VMEM, VMEM], [rows(512)])
    bundle = crossed(bundle, "core", 2, 1)
    second = crossed(mine[2], "core", 2, 1)
    part = scatter(part, ([(0, a)], mine[1]), ([(0, b)], mine[2]))
    last = crossed(relay(part, mine[3], LONG), "core", 2, 1)
    part = scatter(part, ([(0, c)], mine[3]), ([(1, b)], second), ([(1, 0), (1, a)], bundle))
    part = scatter(part, ([(1, c)], last))
    (solved,) = call(solve_kernel, [part.reshape(2048, LANES), first_half, second_half], [VMEM] * 3, [rows(256)], mib=16)

    blocks = {0: solved, **{d: crossed(solved, "chip", 4, d) for d in OTHERS}}
    other_blocks = [blocks[d] for d in OTHERS]
    own_swapped = crossed(solved, "core", 2, 1)

    panels = [ph, pl_, derivative_packed]

    def half_of(members, blocks):
        width = len(members) * LANES
        return call(
            functools.partial(half_kernel, members), [*panels, *blocks], [VMEM] * (3 + len(blocks)),
            [sds((2, 256, width), F32), rows(8)], [buffer(256, width, dtype=BF16)] * 2, mib=8,
            cost=(len(members) * (50 << 20), 2 << 20),
        )

    def rest_of(members, halves, theirs, before=()):
        count = len(members)
        return call(
            functools.partial(rest_kernel, members), [*panels, *halves, theirs, *before],
            [VMEM] * 6 + [ANY] * len(before), [rows(count * 64 + 8)] * 4,
            [buffer(256, count * LANES, dtype=BF16)] * 2 + [buffer(count, 256, LANES)], mib=8,
            cost=(count * (50 << 20), 2 << 20),
        )

    def exchange(pieces):
        return [pieces[0]] + [shifted(pieces[t], "pcol", 4, t) for t in (1, 2, 3)]

    own_pieces = rest_of((0,), half_of((0,), [solved]), own_swapped)
    own_arrived = exchange(own_pieces)
    own_total = call(
        functools.partial(sum_kernel, 1), own_arrived, [VMEM] * 4, [rows(64), rows(8)],
        [buffer(4, 8, LANES)], cost=LONG,
    )
    (forward,) = call(forward_kernel, [own_pieces[0], *other_blocks], [ANY] + [VMEM] * 3, [rows(768)])
    others_swapped = crossed(forward, "core", 2, 1)
    before = [own_total[0]]
    other_pieces = rest_of(OTHERS, half_of(OTHERS, other_blocks), others_swapped, before)

    (adjoint,) = call(
        adjoint_kernel, [*[blocks[d] for d in range(4)], own_swapped, others_swapped], [VMEM] * 6, [rows(2048)], [buffer(4, 256, LANES)],
        mib=6, cost=(1 << 18, 3 << 20),
    )
    updated, sensitivity = call(
        final_kernel, [to_rows(trailing), *own_total, *exchange(other_pieces)], [VMEM] * 7, [rows(256), rows(2)],
        [buffer(192, LANES), buffer(8, LANES), buffer(4, 8, LANES), buffer(4, 64, LANES), buffer(4, 1, LANES)],
    )
    return (
        from_rows(updated, 64, 2, 256),
        from_rows(adjoint, 512, 2, 256),
        sensitivity.reshape(256),
    )


def complex_product(lhs, rhs):
    rows, _, inner = lhs.shape
    re, im = rhs[:, 0, :], rhs[:, 1, :]
    stacked = jnp.concatenate(
        [jnp.concatenate([re, im], axis=1), jnp.concatenate([-im, re], axis=1)], axis=0
    )
    result = jnp.dot(
        lhs.reshape(rows, 2 * inner), stacked, preferred_element_type=F32, precision=lax.Precision.HIGHEST
    )
    return result.reshape(rows, 2, rhs.shape[2])


def per_device_plain(rhs_panel, pivots, diag_inverse, panel_column, trailing, derivative):
    gathered = lax.all_gather(rhs_panel, ("prow", "pcol"), axis=0, tiled=True)
    solved = complex_product(diag_inverse, jnp.take(gathered, pivots, axis=0))
    correction = lax.psum_scatter(
        complex_product(panel_column, solved), "pcol", scatter_dimension=0, tiled=True
    )
    sensitivity = lax.psum(-jnp.sum(solved * derivative, axis=(0, 1)), "pcol")
    return trailing - correction, solved, sensitivity


def solution(mesh):
    fits = mesh.shape["prow"] == 8 and mesh.shape["pcol"] == 4
    if fits:
        mesh = Mesh(mesh.devices.reshape(4, 2, 4), ("chip", "core", "pcol"))
        row = ("chip", "core")
    else:
        row = ("prow",)
    in_specs = (
        P(row + ("pcol",), None, None),
        P(),
        P("pcol", None, None),
        P(row, None, "pcol"),
        P(row + ("pcol",), None, None),
        P("pcol", None, None),
    )
    out_specs = (P(row + ("pcol",), None, None), P("pcol", None, None), P())
    return jax.shard_map(
        per_device if fits else per_device_plain,
        mesh=mesh, in_specs=in_specs, out_specs=out_specs, check_vma=False,
    )
```

time: 166 us -> 54.2 us (0.33)
  local copies, waits for them, and re-layouts: 68.2 us -> 0.92 us
  other arithmetic: 25.1 us -> 0 us
  starting transfers between devices: 0.08 us -> 23.4 us
  matrix products: 18.6 us -> 0 us
  Pallas kernels: 0 us -> 17.9 us
  waiting for transfers between devices: 27.4 us -> 10.9 us
  between operations: 14.8 us -> 0.86 us
  blocking collectives: 11.1 us -> 0 us
    gather x1 -> x0, local copies, waits for them, and re-layouts: 26.3 us -> none  [per_device(): permuted = jnp.take(diag_inverse, inverse_order, axis=2)]
    unnamed x3 -> x0, waiting for transfers between devices: 24 us -> none
    ppermute x0 -> x20, starting transfers between devices: none -> 23.4 us  [the longest x9 14 us: shifted(): return lax.ppermute(x, axis, [(i, (i + t) % count) for i in range(count)])]
    unnamed x20 -> x10, local copies, waits for them, and re-layouts: 22.6 us -> 0.92 us
    dot_general x2 -> x0, matrix products: 18.6 us -> none  [complex_product(): jnp.dot(flat, stacked, preferred_element_type=jnp.float32, precision=lax....]
    pallas_call x0 -> x19, Pallas kernels: none -> 17.9 us  [call(): pl.pallas_call(kernel, in_specs=in_specs, out_specs=[SMEM if o.dtype == j...]
    psum x1 -> x0, blocking collectives: 11.1 us -> none  [per_device(): sensitivity = lax.psum(local_terms, 'pcol')]
    ppermute x0 -> x20, waiting for transfers between devices: none -> 10.9 us  [the longest x9 9 us: shifted(): return lax.ppermute(x, axis, [(i, (i + t) % count) for i in range(count)])]
  transfers between devices with their start and end apart: 2 -> 20, of which waited for: 2 -> 8; matrix products, arithmetic and copies ran while one was open for 40% -> 0% of each run, Pallas kernels for 0% -> 26%
where the time goes in v1:
time: 54.2 us; the launch traced here: 54 us
  starting transfers between devices  23.4 us (43%)
  Pallas kernels  17.9 us (33%)
  waiting for transfers between devices  10.9 us (20%)
  local copies, waits for them, and re-layouts  0.92 us (2%)
  between operations  0.86 us (2%)
    pallas_call x19, Pallas kernels, call(): pl.pallas_call(kernel, in_specs=in_specs, out_specs=[SMEM if o.dtype == j...  17.9 us
    ppermute x9, starting transfers between devices, shifted(): return lax.ppermute(x, axis, [(i, (i + t) % count) for i in range(count)])  14 us
    ppermute x11, starting transfers between devices, crossed(): return lax.ppermute(x, axis, [(i, i ^ d) for i in range(count)])  9.34 us
    ppermute x9, waiting for transfers between devices, shifted(): return lax.ppermute(x, axis, [(i, (i + t) % count) for i in range(count)])  9 us
    ppermute x11, waiting for transfers between devices, crossed(): return lax.ppermute(x, axis, [(i, i ^ d) for i in range(count)])  1.94 us
  transfers between devices with their start and end apart: 20, of which 8 were waited for; matrix products, arithmetic and copies ran while one was open for 0% of the time, Pallas kernels for 26%

profile of v1, /device:TPU:0, one launch (start us, length us, event | category | flops | bytes accessed | tf_op | source)
XLA Modules:
  0.0 54.0 jit_solution(14927010233424711382)
XLA Ops:
  0.6 0.9 %copy-done.4 = f32[64,2,256]{2,1,0:T(2,128)S(1)} copy-done((f32[64,2,256]{2,1,0:T(2,128)S(1)}, f32[64,2,256]{2,1,0:T(2,128)}, u32[]{:S(2)}) %copy-start.4) | copy-done | bytes 131096
  1.7 4.0 %collective-permute-start = (f32[64,128]{1,0:T(8,128)S(1)}, f32[64,128]{1,0:T(8,128)S(1)}, u32[]{:S(2)}, u32[]{:S(2)}) collective-permute-start(f32[64,128]{1,0:T(8,128)S(1)} %get-tuple-element.33), channel_id=1, source_target_pairs={{0,24},{8,16},{16,8},{24,0},{1,25},{9,17},{17,9},{25,1},{2,26},{10... | collective-permute-start | bytes 98312 | tf_op jit(solution)/shard_map/ppermute | solution.py:285
  5.6 0.5 collective-permute-start.1
  6.3 1.9 %shard_map.86.after_ref.first_ref = bf16[512,2048]{1,0:T(8,128)(2,1)S(1)} custom-call(f32[512,32,128]{2,1,0:T(8,128)} %bitcast.62), custom_call_target="tpu_custom_call" | custom-call | flops 4194304 | bytes 4194304 | tf_op jit(solution)/shard_map/pallas_call | solution.py:293
  8.1 1.4 %collective-permute-done.1.b1 = f32[64,128]{1,0:T(8,128)S(1)} collective-permute-done((f32[64,128]{1,0:T(8,128)S(1)}, f32[64,128]{1,0:T(8,128)S(1)}, u32[]{:S(2)}, u32[]{:S(2)}) %collective-permute-start.1) | collective-permute-done | bytes 32800 | tf_op jit(solution)/shard_map/ppermute | solution.py:285
  9.5 0.5 collective-permute-done.2.b2
  10.1 1.6 %collective-permute-start.3 = (f32[256,128]{1,0:T(8,128)S(1)}, f32[256,128]{1,0:T(8,128)S(1)}, u32[]{:S(2)}, u32[]{:S(2)}) collective-permute-start(f32[256,128]{1,0:T(8,128)S(1)} %shard_map.88.a_ref), channel_id=1, source_target_pairs={{0,1},{1,2},{2,3},{3,0},{4,5},{5,6},{6,7},{7,4},{8,9},{9,10},{10,1... | collective-permute-start | bytes 393224 | tf_op jit(solution)/shard_map/ppermute | solution.py:289
  11.7 2.2 %collective-permute-start.4 = (f32[256,128]{1,0:T(8,128)S(1)}, f32[256,128]{1,0:T(8,128)S(1)}, u32[]{:S(2)}, u32[]{:S(2)}) collective-permute-start(f32[256,128]{1,0:T(8,128)S(1)} %shard_map.88.a_ref), channel_id=1, source_target_pairs={{0,3},{1,0},{2,1},{3,2},{4,7},{5,4},{6,5},{7,6},{8,11},{9,8},{10,9... | collective-permute-start | bytes 393224 | tf_op jit(solution)/shard_map/ppermute | solution.py:289
  14.0 0.8 %collective-permute-start.5 = (f32[256,128]{1,0:T(8,128)S(1)}, f32[256,128]{1,0:T(8,128)S(1)}, u32[]{:S(2)}, u32[]{:S(2)}) collective-permute-start(f32[256,128]{1,0:T(8,128)S(1)} %shard_map.88.a_ref), channel_id=1, source_target_pairs={{0,2},{1,3},{2,0},{3,1},{4,6},{5,7},{6,4},{7,5},{8,10},{9,11},{10,... | collective-permute-start | bytes 393224 | tf_op jit(solution)/shard_map/ppermute | solution.py:289
  14.8 4.8 %shard_map.89 = (bf16[512,2048]{1,0:T(8,128)(2,1)S(1)}, s32[2048]{0:T(1024)S(1)}, f32[2048,1,128]{2,1,0:T(1,128)S(1)}) custom-call(s32[2048]{0:T(1024)S(1)} %copy-done.3, f32[512,32,128]{2,1,0:T(8,128)} %bitcast.63, f32[256,1,128]{2,1,0:T(1,128)S(1)} %bitcast.53), custom_call_target="tpu_custom_call" | custom-call | flops 4194304 | bytes 4194304 | tf_op jit(solution)/shard_map/pallas_call | solution.py:293
  19.7 0.5 collective-permute-start.6
  20.2 1.4 %shard_map.90.part_hbm.after_ref = f32[2048,1,128]{2,1,0:T(1,128)S(1)} custom-call(s32[2048]{0:T(1024)S(1)} %get-tuple-element.36.inverse_hbm, f32[2048,1,128]{2,1,0:T(1,128)S(1)} %get-tuple-element.37.part_hbm, f32[256,1,128]{2,1,0:T(1,128)S(1)} %bitcast.54, f32[256,1,128]{2,1,0:T(1,128)S(1)} %bitcast.57), custom_call_target="tpu_custom_call" | custom-call | flops 1048576 | bytes 1048576 | tf_op jit(solution)/shard_map/pallas_call | solution.py:293
  21.6 2.6 %collective-permute-done.5.x_ref = f32[256,128]{1,0:T(8,128)S(1)} collective-permute-done((f32[256,128]{1,0:T(8,128)S(1)}, f32[256,128]{1,0:T(8,128)S(1)}, u32[]{:S(2)}, u32[]{:S(2)}) %collective-permute-start.5) | collective-permute-done | bytes 131104 | tf_op jit(solution)/shard_map/ppermute | solution.py:289
  24.3 2.1 %shard_map.92.part_hbm = f32[2048,1,128]{2,1,0:T(1,128)S(1)} custom-call(s32[2048]{0:T(1024)S(1)} %get-tuple-element.36.inverse_hbm, f32[2048,1,128]{2,1,0:T(1,128)S(1)} %shard_map.90.part_hbm.after_ref, f32[256,1,128]{2,1,0:T(1,128)S(1)} %bitcast.56, f32[256,1,128]{2,1,0:T(1,128)S(1)} %bitcast.58, f32[512,1,128]{2,1,0:T(1,128)S(1)} %bitcast.55), custom_call_target="tpu_custom_call" | custom-call | flops 1048576 | bytes 1048576 | tf_op jit(solution)/shard_map/pallas_call | solution.py:293
  26.4 1.0 %shard_map.94 = f32[2048,1,128]{2,1,0:T(1,128)S(1)} custom-call(s32[2048]{0:T(1024)S(1)} %get-tuple-element.36.inverse_hbm, f32[2048,1,128]{2,1,0:T(1,128)S(1)} %shard_map.92.part_hbm, f32[256,1,128]{2,1,0:T(1,128)S(1)} %bitcast.59), custom_call_target="tpu_custom_call" | custom-call | flops 1048576 | bytes 1048576 | tf_op jit(solution)/shard_map/pallas_call | solution.py:293
  27.4 1.3 %shard_map.95.rest_0_.m0 = f32[256,128]{1,0:T(8,128)S(1)} custom-call(f32[2048,128]{1,0:T(8,128)S(1)} %bitcast.50, bf16[512,2048]{1,0:T(8,128)(2,1)S(1)} %shard_map.86.after_ref.first_ref, bf16[512,2048]{1,0:T(8,128)(2,1)S(1)} %get-tuple-element.38.after_ref.second_ref), custom_call_target="tpu_custom_call" | custom-call | tf_op jit(solution)/shard_map/pallas_call | solution.py:293
  28.8 0.5 %collective-permute-start.9 = (f32[256,128]{1,0:T(8,128)S(1)}, f32[256,128]{1,0:T(8,128)S(1)}, u32[]{:S(2)}, u32[]{:S(2)}) collective-permute-start(f32[256,128]{1,0:T(8,128)S(1)} %shard_map.95.rest_0_.m0), channel_id=1, source_target_pairs={{0,4},{4,0},{1,5},{5,1},{2,6},{6,2},{3,7},{7,3},{8,12},{12,8},{9,1... | collective-permute-start | bytes 393224 | tf_op jit(solution)/shard_map/ppermute | solution.py:285
  29.3 1.7 %collective-permute-start.13 = (f32[256,128]{1,0:T(8,128)S(1)}, f32[256,128]{1,0:T(8,128)S(1)}, u32[]{:S(2)}, u32[]{:S(2)}) collective-permute-start(f32[256,128]{1,0:T(8,128)S(1)} %shard_map.95.rest_0_.m0), channel_id=1, source_target_pairs={{0,24},{8,16},{16,8},{24,0},{1,25},{9,17},{17,9},{25,1},{2,26},{10... | collective-permute-start | bytes 393224 | tf_op jit(solution)/shard_map/ppermute | solution.py:285
  31.0 0.5 collective-permute-start.14
  31.5 1.3 %collective-permute-start.15 = (f32[256,128]{1,0:T(8,128)S(1)}, f32[256,128]{1,0:T(8,128)S(1)}, u32[]{:S(2)}, u32[]{:S(2)}) collective-permute-start(f32[256,128]{1,0:T(8,128)S(1)} %shard_map.95.rest_0_.m0), channel_id=1, source_target_pairs={{0,16},{8,24},{16,0},{24,8},{1,17},{9,25},{17,1},{25,9},{2,18},{10... | collective-permute-start | bytes 393224 | tf_op jit(solution)/shard_map/ppermute | solution.py:285
  32.8 0.7 %shard_map.85 = (bf16[2,256,512]{2,1,0:T(8,128)(2,1)S(1)}, bf16[2,256,512]{2,1,0:T(8,128)(2,1)S(1)}, f32[4,512,128]{2,1,0:T(8,128)S(1)}) custom-call(f32[2048,128]{1,0:T(8,128)S(1)} %bitcast.51, f32[2048,128]{1,0:T(8,128)S(1)} %bitcast.52), custom_call_target="tpu_custom_call" | custom-call | flops 2097152 | bytes 4194304 | tf_op jit(solution)/shard_map/pallas_call | solution.py:293
  34.3 0.7 %collective-permute-start.10 = (f32[72,128]{1,0:T(8,128)S(1)}, f32[72,128]{1,0:T(8,128)S(1)}, u32[]{:S(2)}, u32[]{:S(2)}) collective-permute-start(f32[72,128]{1,0:T(8,128)S(1)} %get-tuple-element.42), channel_id=1, source_target_pairs={{0,1},{1,2},{2,3},{3,0},{4,5},{5,6},{6,7},{7,4},{8,9},{9,10},{10,1... | collective-permute-start | bytes 110600 | tf_op jit(solution)/shard_map/ppermute | solution.py:289
  35.1 2.1 %collective-permute-start.11 = (f32[72,128]{1,0:T(8,128)S(1)}, f32[72,128]{1,0:T(8,128)S(1)}, u32[]{:S(2)}, u32[]{:S(2)}) collective-permute-start(f32[72,128]{1,0:T(8,128)S(1)} %get-tuple-element.43), channel_id=1, source_target_pairs={{0,2},{1,3},{2,0},{3,1},{4,6},{5,7},{6,4},{7,5},{8,10},{9,11},{10,... | collective-permute-start | bytes 110600 | tf_op jit(solution)/shard_map/ppermute | solution.py:289
  37.2 2.1 %collective-permute-start.12 = (f32[72,128]{1,0:T(8,128)S(1)}, f32[72,128]{1,0:T(8,128)S(1)}, u32[]{:S(2)}, u32[]{:S(2)}) collective-permute-start(f32[72,128]{1,0:T(8,128)S(1)} %get-tuple-element.44), channel_id=1, source_target_pairs={{0,3},{1,0},{2,1},{3,2},{4,7},{5,4},{6,5},{7,6},{8,11},{9,8},{10,9... | collective-permute-start | bytes 110600 | tf_op jit(solution)/shard_map/ppermute | solution.py:289
  39.4 0.6 %shard_map.99 = (f32[2,256,384]{2,1,0:T(8,128)S(1)}, f32[8,128]{1,0:T(8,128)S(1)}) custom-call(bf16[2,256,512]{2,1,0:T(8,128)(2,1)S(1)} %get-tuple-element.29.ph_ref, bf16[2,256,512]{2,1,0:T(8,128)(2,1)S(1)} %get-tuple-element.30.pl_ref, f32[4,512,128]{2,1,0:T(8,128)S(1)} %get-tuple-element.31.derivative_ref, ...), custom_call_target="tpu_custom_call" | custom-call | flops 157286400 | bytes 2097152 | tf_op jit(solution)/shard_map/pallas_call | solution.py:293
  41.2 0.8 %shard_map.101 = (f32[200,128]{1,0:T(8,128)S(1)}, f32[200,128]{1,0:T(8,128)S(1)}, f32[200,128]{1,0:T(8,128)S(1)}, f32[200,128]{1,0:T(8,128)S(1)}) custom-call(bf16[2,256,512]{2,1,0:T(8,128)(2,1)S(1)} %get-tuple-element.29.ph_ref, bf16[2,256,512]{2,1,0:T(8,128)(2,1)S(1)} %get-tuple-element.30.pl_ref, f32[4,512,128]{2,1,0:T(8,128)S(1)} %get-tuple-element.31.derivative_ref, ...), custom_call_target="tpu_custom_call" | custom-call | flops 157286400 | bytes 2097152 | tf_op jit(solution)/shard_map/pallas_call | solution.py:293
  42.0 1.7 %collective-permute-start.17 = (f32[200,128]{1,0:T(8,128)S(1)}, f32[200,128]{1,0:T(8,128)S(1)}, u32[]{:S(2)}, u32[]{:S(2)}) collective-permute-start(f32[200,128]{1,0:T(8,128)S(1)} %get-tuple-element.50), channel_id=1, source_target_pairs={{0,1},{1,2},{2,3},{3,0},{4,5},{5,6},{6,7},{7,4},{8,9},{9,10},{10,1... | collective-permute-start | bytes 307208 | tf_op jit(solution)/shard_map/ppermute | solution.py:289
  43.7 2.8 %collective-permute-start.18 = (f32[200,128]{1,0:T(8,128)S(1)}, f32[200,128]{1,0:T(8,128)S(1)}, u32[]{:S(2)}, u32[]{:S(2)}) collective-permute-start(f32[200,128]{1,0:T(8,128)S(1)} %get-tuple-element.51), channel_id=1, source_target_pairs={{0,2},{1,3},{2,0},{3,1},{4,6},{5,7},{6,4},{7,5},{8,10},{9,11},{10,... | collective-permute-start | bytes 307208 | tf_op jit(solution)/shard_map/ppermute | solution.py:289
  46.5 1.4 %shard_map.103 = f32[2048,128]{1,0:T(8,128)} custom-call(f32[256,128]{1,0:T(8,128)S(1)} %shard_map.95.rest_0_.m0, f32[256,128]{1,0:T(8,128)S(1)} %collective-permute-done.14.rest_1_.b1.m1, f32[256,128]{1,0:T(8,128)S(1)} %collective-permute-done.15.rest_2_.b2.m2, f32[256,128]{1,0:T(8,128)S(1)} %collective-permute-done.13.rest_0_.b0.m3, ...), custom_call_target="tpu_custom_call" | custom-call | flops 262144 | bytes 3145728 | tf_op jit(solution)/shard_map/pallas_call | solution.py:293
  47.9 1.8 %collective-permute-done.17.b1 = f32[200,128]{1,0:T(8,128)S(1)} collective-permute-done((f32[200,128]{1,0:T(8,128)S(1)}, f32[200,128]{1,0:T(8,128)S(1)}, u32[]{:S(2)}, u32[]{:S(2)}) %collective-permute-start.17) | collective-permute-done | bytes 102432 | tf_op jit(solution)/shard_map/ppermute | solution.py:289
  49.8 3.4 %collective-permute-done.18.b2 = f32[200,128]{1,0:T(8,128)S(1)} collective-permute-done((f32[200,128]{1,0:T(8,128)S(1)}, f32[200,128]{1,0:T(8,128)S(1)}, u32[]{:S(2)}, u32[]{:S(2)}) %collective-permute-start.18) | collective-permute-done | bytes 102432 | tf_op jit(solution)/shard_map/ppermute | solution.py:289
  53.2 0.8 %shard_map.102 = (f32[256,128]{1,0:T(8,128)}, f32[2,128]{1,0:T(2,128)}) custom-call(f32[256,128]{1,0:T(8,128)S(1)} %bitcast.60, f32[64,128]{1,0:T(8,128)S(1)} %get-tuple-element.45.rest_0_.own_rows, f32[8,128]{1,0:T(8,128)S(1)} %get-tuple-element.46.own_sums, f32[200,128]{1,0:T(8,128)S(1)} %get-tuple-element.49.b0, ...), custom_call_target="tpu_custom_call" | custom-call | tf_op jit(solution)/shard_map/pallas_call | solution.py:293
  (37 shorter events, 2.6 us)
Async XLA Ops:
  0.6 0.9 %copy-start.4 = (f32[64,2,256]{2,1,0:T(2,128)S(1)}, f32[64,2,256]{2,1,0:T(2,128)}, u32[]{:S(2)}) copy-start(f32[64,2,256]{2,1,0:T(2,128)} %param.6) | copy-start | bytes 393220
  1.7 6.5 %collective-permute-start = (f32[64,128]{1,0:T(8,128)S(1)}, f32[64,128]{1,0:T(8,128)S(1)}, u32[]{:S(2)}, u32[]{:S(2)}) collective-permute-start(f32[64,128]{1,0:T(8,128)S(1)} %get-tuple-element.33), channel_id=1, source_target_pairs={{0,24},{8,16},{16,8},{24,0},{1,25},{9,17},{17,9},{25,1},{2,26},{10... | collective-permute-start | bytes 98312 | tf_op jit(solution)/shard_map/ppermute | solution.py:285
  5.6 3.9 %collective-permute-start.1 = (f32[64,128]{1,0:T(8,128)S(1)}, f32[64,128]{1,0:T(8,128)S(1)}, u32[]{:S(2)}, u32[]{:S(2)}) collective-permute-start(f32[64,128]{1,0:T(8,128)S(1)} %get-tuple-element.34), channel_id=1, source_target_pairs={{0,8},{8,0},{16,24},{24,16},{1,9},{9,1},{17,25},{25,17},{2,10},{10... | collective-permute-start | bytes 98312 | tf_op jit(solution)/shard_map/ppermute | solution.py:285
  6.1 3.9 %collective-permute-start.2 = (f32[64,128]{1,0:T(8,128)S(1)}, f32[64,128]{1,0:T(8,128)S(1)}, u32[]{:S(2)}, u32[]{:S(2)}) collective-permute-start(f32[64,128]{1,0:T(8,128)S(1)} %get-tuple-element.35), channel_id=1, source_target_pairs={{0,16},{8,24},{16,0},{24,8},{1,17},{9,25},{17,1},{25,9},{2,18},{10... | collective-permute-start | bytes 98312 | tf_op jit(solution)/shard_map/ppermute | solution.py:285
  10.1 4.7 %copy-start.3 = (s32[2048]{0:T(1024)S(1)}, s32[2048]{0:T(1024)}, u32[]{:S(2)}) copy-start(s32[2048]{0:T(1024)} %pivots_hbm.1) | copy-start | bytes 24580
  10.1 9.5 %collective-permute-start.3 = (f32[256,128]{1,0:T(8,128)S(1)}, f32[256,128]{1,0:T(8,128)S(1)}, u32[]{:S(2)}, u32[]{:S(2)}) collective-permute-start(f32[256,128]{1,0:T(8,128)S(1)} %shard_map.88.a_ref), channel_id=1, source_target_pairs={{0,1},{1,2},{2,3},{3,0},{4,5},{5,6},{6,7},{7,4},{8,9},{9,10},{10,1... | collective-permute-start | bytes 393224 | tf_op jit(solution)/shard_map/ppermute | solution.py:289
  11.7 7.9 %collective-permute-start.4 = (f32[256,128]{1,0:T(8,128)S(1)}, f32[256,128]{1,0:T(8,128)S(1)}, u32[]{:S(2)}, u32[]{:S(2)}) collective-permute-start(f32[256,128]{1,0:T(8,128)S(1)} %shard_map.88.a_ref), channel_id=1, source_target_pairs={{0,3},{1,0},{2,1},{3,2},{4,7},{5,4},{6,5},{7,6},{8,11},{9,8},{10,9... | collective-permute-start | bytes 393224 | tf_op jit(solution)/shard_map/ppermute | solution.py:289
  14.0 10.2 %collective-permute-start.5 = (f32[256,128]{1,0:T(8,128)S(1)}, f32[256,128]{1,0:T(8,128)S(1)}, u32[]{:S(2)}, u32[]{:S(2)}) collective-permute-start(f32[256,128]{1,0:T(8,128)S(1)} %shard_map.88.a_ref), channel_id=1, source_target_pairs={{0,2},{1,3},{2,0},{3,1},{4,6},{5,7},{6,4},{7,5},{8,10},{9,11},{10,... | collective-permute-start | bytes 393224 | tf_op jit(solution)/shard_map/ppermute | solution.py:289
  19.6 4.7 %collective-permute-start.7 = (f32[512,128]{1,0:T(8,128)S(1)}, f32[512,128]{1,0:T(8,128)S(1)}, u32[]{:S(2)}, u32[]{:S(2)}) collective-permute-start(f32[512,128]{1,0:T(8,128)S(1)} %shard_map.91), channel_id=1, source_target_pairs={{0,4},{4,0},{1,5},{5,1},{2,6},{6,2},{3,7},{7,3},{8,12},{12,8},{9,1... | collective-permute-start | bytes 786440 | tf_op jit(solution)/shard_map/ppermute | solution.py:285
  19.7 4.6 %collective-permute-start.6 = (f32[256,128]{1,0:T(8,128)S(1)}, f32[256,128]{1,0:T(8,128)S(1)}, u32[]{:S(2)}, u32[]{:S(2)}) collective-permute-start(f32[256,128]{1,0:T(8,128)S(1)} %collective-permute-done.4), channel_id=1, source_target_pairs={{0,4},{4,0},{1,5},{5,1},{2,6},{6,2},{3,7},{7,3},{8,12},{12,8},{9,1... | collective-permute-start | bytes 393224 | tf_op jit(solution)/shard_map/ppermute | solution.py:285
  24.2 2.2 %collective-permute-start.8 = (f32[256,128]{1,0:T(8,128)S(1)}, f32[256,128]{1,0:T(8,128)S(1)}, u32[]{:S(2)}, u32[]{:S(2)}) collective-permute-start(f32[256,128]{1,0:T(8,128)S(1)} %shard_map.93), channel_id=1, source_target_pairs={{0,4},{4,0},{1,5},{5,1},{2,6},{6,2},{3,7},{7,3},{8,12},{12,8},{9,1... | collective-permute-start | bytes 393224 | tf_op jit(solution)/shard_map/ppermute | solution.py:285
  27.4 5.4 %copy-start = (f32[256,2,512]{2,1,0:T(2,128)S(1)}, f32[256,2,512]{2,1,0:T(2,128)}, u32[]{:S(2)}) copy-start(f32[256,2,512]{2,1,0:T(2,128)} %param.9) | copy-start | bytes 3145732
  27.4 5.4 %copy-start.1 = (f32[512,2,256]{2,1,0:T(2,128)S(1)}, f32[512,2,256]{2,1,0:T(2,128)}, u32[]{:S(2)}) copy-start(f32[512,2,256]{2,1,0:T(2,128)} %param.11) | copy-start | bytes 3145732
  28.8 5.1 %collective-permute-start.9 = (f32[256,128]{1,0:T(8,128)S(1)}, f32[256,128]{1,0:T(8,128)S(1)}, u32[]{:S(2)}, u32[]{:S(2)}) collective-permute-start(f32[256,128]{1,0:T(8,128)S(1)} %shard_map.95.rest_0_.m0), channel_id=1, source_target_pairs={{0,4},{4,0},{1,5},{5,1},{2,6},{6,2},{3,7},{7,3},{8,12},{12,8},{9,1... | collective-permute-start | bytes 393224 | tf_op jit(solution)/shard_map/ppermute | solution.py:285
  29.3 7.8 %collective-permute-start.13 = (f32[256,128]{1,0:T(8,128)S(1)}, f32[256,128]{1,0:T(8,128)S(1)}, u32[]{:S(2)}, u32[]{:S(2)}) collective-permute-start(f32[256,128]{1,0:T(8,128)S(1)} %shard_map.95.rest_0_.m0), channel_id=1, source_target_pairs={{0,24},{8,16},{16,8},{24,0},{1,25},{9,17},{17,9},{25,1},{2,26},{10... | collective-permute-start | bytes 393224 | tf_op jit(solution)/shard_map/ppermute | solution.py:285
  31.0 8.3 %collective-permute-start.14 = (f32[256,128]{1,0:T(8,128)S(1)}, f32[256,128]{1,0:T(8,128)S(1)}, u32[]{:S(2)}, u32[]{:S(2)}) collective-permute-start(f32[256,128]{1,0:T(8,128)S(1)} %shard_map.95.rest_0_.m0), channel_id=1, source_target_pairs={{0,8},{8,0},{16,24},{24,16},{1,9},{9,1},{17,25},{25,17},{2,10},{10... | collective-permute-start | bytes 393224 | tf_op jit(solution)/shard_map/ppermute | solution.py:285
  31.5 7.7 %collective-permute-start.15 = (f32[256,128]{1,0:T(8,128)S(1)}, f32[256,128]{1,0:T(8,128)S(1)}, u32[]{:S(2)}, u32[]{:S(2)}) collective-permute-start(f32[256,128]{1,0:T(8,128)S(1)} %shard_map.95.rest_0_.m0), channel_id=1, source_target_pairs={{0,16},{8,24},{16,0},{24,8},{1,17},{9,25},{17,1},{25,9},{2,18},{10... | collective-permute-start | bytes 393224 | tf_op jit(solution)/shard_map/ppermute | solution.py:285
  34.3 5.9 %collective-permute-start.10 = (f32[72,128]{1,0:T(8,128)S(1)}, f32[72,128]{1,0:T(8,128)S(1)}, u32[]{:S(2)}, u32[]{:S(2)}) collective-permute-start(f32[72,128]{1,0:T(8,128)S(1)} %get-tuple-element.42), channel_id=1, source_target_pairs={{0,1},{1,2},{2,3},{3,0},{4,5},{5,6},{6,7},{7,4},{8,9},{9,10},{10,1... | collective-permute-start | bytes 110600 | tf_op jit(solution)/shard_map/ppermute | solution.py:289
  35.1 5.6 %collective-permute-start.11 = (f32[72,128]{1,0:T(8,128)S(1)}, f32[72,128]{1,0:T(8,128)S(1)}, u32[]{:S(2)}, u32[]{:S(2)}) collective-permute-start(f32[72,128]{1,0:T(8,128)S(1)} %get-tuple-element.43), channel_id=1, source_target_pairs={{0,2},{1,3},{2,0},{3,1},{4,6},{5,7},{6,4},{7,5},{8,10},{9,11},{10,... | collective-permute-start | bytes 110600 | tf_op jit(solution)/shard_map/ppermute | solution.py:289
  37.2 4.0 %collective-permute-start.12 = (f32[72,128]{1,0:T(8,128)S(1)}, f32[72,128]{1,0:T(8,128)S(1)}, u32[]{:S(2)}, u32[]{:S(2)}) collective-permute-start(f32[72,128]{1,0:T(8,128)S(1)} %get-tuple-element.44), channel_id=1, source_target_pairs={{0,3},{1,0},{2,1},{3,2},{4,7},{5,4},{6,5},{7,6},{8,11},{9,8},{10,9... | collective-permute-start | bytes 110600 | tf_op jit(solution)/shard_map/ppermute | solution.py:289
  39.3 1.9 %collective-permute-start.16 = (f32[768,128]{1,0:T(8,128)S(1)}, f32[768,128]{1,0:T(8,128)S(1)}, u32[]{:S(2)}, u32[]{:S(2)}) collective-permute-start(f32[768,128]{1,0:T(8,128)S(1)} %shard_map.100), channel_id=1, source_target_pairs={{0,4},{4,0},{1,5},{5,1},{2,6},{6,2},{3,7},{7,3},{8,12},{12,8},{9,1... | collective-permute-start | bytes 1179656 | tf_op jit(solution)/shard_map/ppermute | solution.py:285
  41.2 12.0 %copy-start.2 = (f32[64,2,256]{2,1,0:T(2,128)S(1)}, f32[64,2,256]{2,1,0:T(2,128)}, u32[]{:S(2)}) copy-start(f32[64,2,256]{2,1,0:T(2,128)} %param.10) | copy-start | bytes 393220
  42.0 7.7 %collective-permute-start.17 = (f32[200,128]{1,0:T(8,128)S(1)}, f32[200,128]{1,0:T(8,128)S(1)}, u32[]{:S(2)}, u32[]{:S(2)}) collective-permute-start(f32[200,128]{1,0:T(8,128)S(1)} %get-tuple-element.50), channel_id=1, source_target_pairs={{0,1},{1,2},{2,3},{3,0},{4,5},{5,6},{6,7},{7,4},{8,9},{9,10},{10,1... | collective-permute-start | bytes 307208 | tf_op jit(solution)/shard_map/ppermute | solution.py:289
  43.7 9.5 %collective-permute-start.18 = (f32[200,128]{1,0:T(8,128)S(1)}, f32[200,128]{1,0:T(8,128)S(1)}, u32[]{:S(2)}, u32[]{:S(2)}) collective-permute-start(f32[200,128]{1,0:T(8,128)S(1)} %get-tuple-element.51), channel_id=1, source_target_pairs={{0,2},{1,3},{2,0},{3,1},{4,6},{5,7},{6,4},{7,5},{8,10},{9,11},{10,... | collective-permute-start | bytes 307208 | tf_op jit(solution)/shard_map/ppermute | solution.py:289
  46.5 6.7 %collective-permute-start.19 = (f32[200,128]{1,0:T(8,128)S(1)}, f32[200,128]{1,0:T(8,128)S(1)}, u32[]{:S(2)}, u32[]{:S(2)}) collective-permute-start(f32[200,128]{1,0:T(8,128)S(1)} %get-tuple-element.52), channel_id=1, source_target_pairs={{0,3},{1,0},{2,1},{3,2},{4,7},{5,4},{6,5},{7,6},{8,11},{9,8},{10,9... | collective-permute-start | bytes 307208 | tf_op jit(solution)/shard_map/ppermute | solution.py:289
